TPU v7x, 1024 devices: a whole 8x8x8 slice. The times are simulated.
1024 devices in a mesh: dp: 8 (over z), row: 8 (over x), col: 16 (over y, core).
Axes of the slice: x: 8, y: 8, z: 8, core: 2. Of those that a mesh axis runs over, the one named last changes fastest.
Arguments:
- grad: bfloat16 [8, 4096, 14336], P('dp', 'row', 'col'), may hold values from -6 to 6
- error: bfloat16 [8, 4096, 14336], P('dp', 'row', 'col'), may hold values from -6 to 6
- q_init: float32 [14336, 128], P('col'), may hold values from -6 to 6
Outputs:
- new_error: bfloat16 [8, 4096, 14336], P('dp', 'row', 'col')
- q_factor: float32 [14336, 128], P('col')
All inputs are finite; a program needn't handle non-finite values.
Results may differ from a plain program's by a relative error of at most 0.001.
Values sent between devices are 32-bit elements; how exact they have to be, the bound alone decides.
No kernel may reach another device: no remote copies, remote signals or barrier semaphores. Data moves between devices by JAX's collectives and lax.ppermute only.
A program may use at most 32 MiB of HBM per device.

v0:
```python
import functools

import jax
import jax.numpy as jnp
from jax import lax
from jax.experimental import pallas as pl
from jax.experimental.pallas import tpu as pltpu
from jax.sharding import Mesh
from jax.sharding import PartitionSpec as P

HIGHEST = lax.Precision.HIGHEST
BLOCK = 32
VMEM_LIMIT = 24 * 2**20


def mm(a, b, on_a, on_b):
    return lax.dot_general(
        a,
        b,
        (((on_a,), (on_b,)), ((), ())),
        precision=HIGHEST,
        preferred_element_type=jnp.float32,
    )


def mm16(a, b):
    return jnp.dot(a, b, preferred_element_type=jnp.float32)


def three_parts(x):
    first = x.astype(jnp.bfloat16)
    rest = x - first.astype(jnp.float32)
    second = rest.astype(jnp.bfloat16)
    third = (rest - second.astype(jnp.float32)).astype(jnp.bfloat16)
    return first, second, third


def add_parts(x, axis):
    n = x.shape[axis] // 3
    a, b, c = (lax.slice_in_dim(x, i * n, (i + 1) * n, axis=axis) for i in range(3))
    return a + (b + c)


def diagonal(gram, axis):
    n = gram.shape[0]
    row = lax.broadcasted_iota(jnp.int32, (n, n), 0)
    lane = lax.broadcasted_iota(jnp.int32, (n, n), 1)
    return jnp.sum(jnp.where(row == lane, gram, 0.0), axis=axis, keepdims=True)


def small_inverse(block, width):
    n = block.shape[0]
    row = lax.broadcasted_iota(jnp.int32, (n, width), 0)
    lane = lax.broadcasted_iota(jnp.int32, (n, width), 1)
    inv = jnp.where(row == lane, 1.0, 0.0)
    cols = [jnp.broadcast_to(block[:, k : k + 1], (n, width)) for k in range(n)]
    for k in range(n):
        scale = lax.rsqrt(cols[k][k : k + 1, :])
        lower = cols[k] * scale
        pivot = inv[k : k + 1, :] * scale
        inv = jnp.where(
            row > k,
            inv - lower * pivot,
            jnp.where(row == k, jnp.broadcast_to(pivot, (n, width)), inv),
        )
        for j in range(k + 1, n):
            low = (j // 8) * 8
            new = cols[j][low:, :] - lower[low:, :] * lower[j : j + 1, :]
            cols[j] = new if low == 0 else jnp.concatenate([cols[j][:low, :], new], axis=0)
    return inv


def lower_inverse(gram):
    n = gram.shape[0]
    row = lax.broadcasted_iota(jnp.int32, (n, n), 0)
    lane = lax.broadcasted_iota(jnp.int32, (n, n), 1)
    left, right = gram, jnp.where(row == lane, 1.0, 0.0)
    out = []
    for start in range(0, n, BLOCK):
        small = small_inverse(left[:BLOCK, start : start + BLOCK], n)[:, :BLOCK]
        new_right = mm(small, right[:BLOCK, :], 1, 0)
        out.append(new_right)
        if start + BLOCK < n:
            new_left = mm(small, left[:BLOCK, :], 1, 0)
            below = new_left[:, start + BLOCK :]
            left = left[BLOCK:, :] - mm(below, new_left, 0, 0)
            right = right[BLOCK:, :] - mm(below, new_right, 0, 0)
    return jnp.concatenate(out, axis=0)


def left_product(grad, error, q_mat, scale):
    parts = jnp.concatenate(three_parts(q_mat), axis=1)
    return add_parts(mm16(grad, parts) + mm16(error, parts), 1) * scale


def first_left_kernel(scale, grad, error, q_mat, out):
    out[...] = left_product(grad[0], error[0], q_mat[...], scale)


def next_left_kernel(scale, grad, error, both, out):
    cols = grad.shape[2]
    both = both[...].reshape(-1, both.shape[2])
    q_mat = both[:cols] * lax.rsqrt(diagonal(both[cols:], 0))
    out[...] = left_product(grad[0], error[0], q_mat, scale)


def right_kernel(scale, grad, error, p_mat, out):
    p_mat = p_mat[...].reshape(-1, p_mat.shape[2])
    p_t = p_mat.T
    parts = jnp.concatenate(three_parts(p_t), axis=0)
    term = add_parts(mm16(parts, grad[0]) + mm16(parts, error[0]), 0).T
    gram = mm(p_t, p_mat, 1, 0)
    both = jnp.concatenate([term, gram], axis=0) * scale
    out[...] = both.reshape(out.shape)


def sum_kernel(pieces, out):
    out[...] = jnp.broadcast_to(jnp.sum(pieces[...], axis=0)[None], out.shape)


def sum_scale_kernel(pieces, inverse, out):
    piece = mm(jnp.sum(pieces[...], axis=0), inverse[...], 1, 1)
    out[...] = jnp.broadcast_to(piece[None], out.shape)


def inverse_kernel(both, out):
    n = out.shape[0]
    gram = both[...].reshape(-1, n)[-n:]
    by_row = lax.rsqrt(diagonal(gram, 1))
    by_lane = lax.rsqrt(diagonal(gram, 0))
    out[...] = lower_inverse(gram * by_row * by_lane)


def last_kernel(grad, error, p_mat, both, new_error, q_factor):
    cols = grad.shape[2]
    p_mat = p_mat[...].reshape(-1, p_mat.shape[2])
    both = both[...].reshape(-1, both.shape[2])
    inverse = lower_inverse(both[cols:])
    q_mat = mm(both[:cols], inverse, 1, 1)
    q_factor[...] = q_mat
    p_hat = mm(p_mat, inverse, 1, 1)
    approx = mm(p_hat, q_mat, 1, 1)
    comp = grad[0].astype(jnp.float32) + error[0].astype(jnp.float32)
    new_error[0] = (comp - approx).astype(jnp.bfloat16)


def call(kernel, shapes, *operands, flops=10**8):
    n_bytes = sum(x.size * x.dtype.itemsize for x in operands)
    single = not isinstance(shapes, tuple)
    outs = (shapes,) if single else shapes
    result = pl.pallas_call(
        kernel,
        out_shape=shapes,
        in_specs=[pl.BlockSpec(memory_space=pltpu.VMEM)] * len(operands),
        out_specs=jax.tree.map(lambda _: pl.BlockSpec(memory_space=pltpu.VMEM), shapes),
        compiler_params=pltpu.CompilerParams(vmem_limit_bytes=VMEM_LIMIT),
        cost_estimate=pl.CostEstimate(
            flops=flops, bytes_accessed=n_bytes + sum(s.size * 4 for s in outs), transcendentals=0
        ),
    )(*operands)
    return result


def f32(*shape):
    return jax.ShapeDtypeStruct(shape, jnp.float32)


def exchange(x, axes):
    return lax.all_to_all(x, axes, 0, 0, tiled=True)


def shards(grad, error, q_init):
    rows, cols = grad.shape[1:]
    rank = q_init.shape[1]
    scale = 1.0 / lax.axis_size("dp")
    left_axes, right_axes = ("dp", "y"), ("dp", "row")
    n_left, n_right = lax.axis_size(left_axes), lax.axis_size(right_axes)
    left_shape = f32(n_left, rows // n_left, rank)
    right_shape = f32(n_right, (cols + rank) // n_right, rank)

    def left_pieces(partial):
        chip = lax.all_gather(partial, "core").sum(axis=0)
        return exchange(chip.reshape(left_shape.shape), left_axes)

    def right_total(p_all):
        partial = call(functools.partial(right_kernel, scale), right_shape, grad, error, p_all)
        pieces = exchange(partial, right_axes)
        return exchange(call(sum_kernel, right_shape, pieces), right_axes)

    partial = call(
        functools.partial(first_left_kernel, scale), f32(rows, rank), grad, error, q_init
    )
    pieces = left_pieces(partial)
    p_all = exchange(call(sum_kernel, left_shape, pieces), left_axes)
    both = right_total(p_all)
    partial = call(functools.partial(next_left_kernel, scale), f32(rows, rank), grad, error, both)
    inverse = call(inverse_kernel, f32(rank, rank), both, flops=4 * 10**9)
    pieces = left_pieces(partial)
    p_all = exchange(call(sum_scale_kernel, left_shape, pieces, inverse), left_axes)
    both = right_total(p_all)
    return call(
        last_kernel,
        (jax.ShapeDtypeStruct(grad.shape, jnp.bfloat16), f32(cols, rank)),
        grad,
        error,
        p_all,
        both,
    )


def solution(mesh):
    size = mesh.devices.shape
    fine = Mesh(mesh.devices.reshape(*size[:2], size[2] // 2, 2), ("dp", "row", "y", "core"))
    block = P("dp", "row", ("y", "core"))
    right = P(("y", "core"), None)
    return jax.shard_map(
        shards, mesh=fine, in_specs=(block, block, right), out_specs=(block, right), check_vma=False
    )
```

profile of v0, /device:TPU:16, one launch (start us, length us, event | category | flops | bytes accessed | tf_op | source)
XLA Modules:
  0.0 210.9 jit_solution(5308980922288218968)
XLA Ops:
  0.6 0.0 copy-start
  0.6 1.2 copy-done
  1.8 0.0 copy-start.2
  1.8 1.2 copy-done.2
  3.0 0.0 copy-start.4
  3.0 1.0 copy-done.4
  4.0 1.2 shard_map.50
  5.2 2.2 %all-gather = f32[1024,128]{1,0:T(8,128)S(1)} all-gather(f32[512,128]{1,0:T(8,128)S(1)} %shard_map.50), channel_id=2, replica_groups=mesh['dp'=8,'row'=8,'y'=8,'core'=2] {'core'}, dimensions={0}, use_global_device_ids=true | all-gather | bytes 786432 | tf_op jit(solution)/shard_map/all_gather | solution.py:182
  7.4 0.0 copy-start.3
  7.4 0.0 copy-start.1
  7.4 37.8 %all_to_all.40.pieces = f32[64,8,128]{2,1,0:T(8,128)S(1)} all-to-all(f32[64,8,128]{2,1,0:T(8,128)S(1)} %bitcast.6), channel_id=1, replica_groups=mesh['dp'=8,'row'=8,'y'=8,'core'=2] {'dp','y'}, dimensions={0} | all-to-all | bytes 524288 | tf_op jit(solution)/shard_map/all_to_all | solution.py:169
  45.3 0.1 shard_map.51
  45.4 18.3 %all_to_all.41.p_mat = f32[64,8,128]{2,1,0:T(8,128)S(1)} all-to-all(f32[64,8,128]{2,1,0:T(8,128)S(1)} %shard_map.51), channel_id=1, replica_groups=mesh['dp'=8,'row'=8,'y'=8,'core'=2] {'dp','y'}, dimensions={0} | all-to-all | bytes 524288 | tf_op jit(solution)/shard_map/all_to_all | solution.py:169
  63.7 0.0 copy-done.3
  63.7 0.0 copy-done.1
  63.7 1.2 shard_map.52
  64.9 26.0 %all_to_all.42.pieces = f32[64,16,128]{2,1,0:T(8,128)S(1)} all-to-all(f32[64,16,128]{2,1,0:T(8,128)S(1)} %shard_map.52), channel_id=1, replica_groups=mesh['dp'=8,'row'=8,'y'=8,'core'=2] {'dp','row'}, dimensions={0} | all-to-all | bytes 1048576 | tf_op jit(solution)/shard_map/all_to_all | solution.py:169
  91.0 0.1 shard_map.53
  91.1 21.9 %all_to_all.43.both = f32[64,16,128]{2,1,0:T(8,128)S(1)} all-to-all(f32[64,16,128]{2,1,0:T(8,128)S(1)} %shard_map.53), channel_id=1, replica_groups=mesh['dp'=8,'row'=8,'y'=8,'core'=2] {'dp','row'}, dimensions={0} | all-to-all | bytes 1048576 | tf_op jit(solution)/shard_map/all_to_all | solution.py:169
  113.0 1.2 shard_map.54
  114.2 2.2 %all-gather.1 = f32[1024,128]{1,0:T(8,128)S(1)} all-gather(f32[512,128]{1,0:T(8,128)S(1)} %shard_map.54), channel_id=3, replica_groups=mesh['dp'=8,'row'=8,'y'=8,'core'=2] {'core'}, dimensions={0}, use_global_device_ids=true | all-gather | bytes 786432 | tf_op jit(solution)/shard_map/all_gather | solution.py:182
  116.4 0.7 reduce_sum.19
  117.2 7.9 %all-to-all-start.4 = ((f32[64,8,128]{2,1,0:T(8,128)}), f32[64,8,128]{2,1,0:T(8,128)S(1)}, u32[]{:S(2)}, u32[]{:S(2)}) async-start(f32[64,8,128]{2,1,0:T(8,128)} %bitcast.3), calls=%async_computation.4 | async-start | bytes 524288 | tf_op jit(solution)/shard_map/all_to_all | solution.py:169
  125.1 4.5 %shard_map.55.inverse = f32[128,128]{1,0:T(8,128)S(1)} custom-call(f32[64,16,128]{2,1,0:T(8,128)S(1)} %all_to_all.43.both), custom_call_target="tpu_custom_call" | custom-call | flops 4000000000 | bytes 589824 | tf_op jit(solution)/shard_map/pallas_call | solution.py:151
  129.6 10.1 %all-to-all-done.4.pieces = f32[64,8,128]{2,1,0:T(8,128)S(1)} async-done(((f32[64,8,128]{2,1,0:T(8,128)}), f32[64,8,128]{2,1,0:T(8,128)S(1)}, u32[]{:S(2)}, u32[]{:S(2)}) %all-to-all-start.4) | async-done | bytes 262176 | tf_op jit(solution)/shard_map/all_to_all | solution.py:169
  139.7 0.3 shard_map.56
  140.0 18.4 %all_to_all.44.p_mat = f32[64,8,128]{2,1,0:T(8,128)S(1)} all-to-all(f32[64,8,128]{2,1,0:T(8,128)S(1)} %shard_map.56), channel_id=1, replica_groups=mesh['dp'=8,'row'=8,'y'=8,'core'=2] {'dp','y'}, dimensions={0} | all-to-all | bytes 524288 | tf_op jit(solution)/shard_map/all_to_all | solution.py:169
  158.4 1.2 shard_map.57
  159.6 21.8 %all_to_all.45.pieces = f32[64,16,128]{2,1,0:T(8,128)S(1)} all-to-all(f32[64,16,128]{2,1,0:T(8,128)S(1)} %shard_map.57), channel_id=1, replica_groups=mesh['dp'=8,'row'=8,'y'=8,'core'=2] {'dp','row'}, dimensions={0} | all-to-all | bytes 1048576 | tf_op jit(solution)/shard_map/all_to_all | solution.py:169
  181.4 0.1 shard_map.58
  181.5 22.2 %all_to_all.46.both = f32[64,16,128]{2,1,0:T(8,128)S(1)} all-to-all(f32[64,16,128]{2,1,0:T(8,128)S(1)} %shard_map.58), channel_id=1, replica_groups=mesh['dp'=8,'row'=8,'y'=8,'core'=2] {'dp','row'}, dimensions={0} | all-to-all | bytes 1048576 | tf_op jit(solution)/shard_map/all_to_all | solution.py:169
  203.7 7.2 %shard_map.59 = (bf16[1,512,896]{2,1,0:T(8,128)(2,1)}, f32[896,128]{1,0:T(8,128)}) custom-call(bf16[1,512,896]{2,1,0:T(8,128)(2,1)S(1)} %copy-done.1, bf16[1,512,896]{2,1,0:T(8,128)(2,1)S(1)} %copy-done.3, f32[64,8,128]{2,1,0:T(8,128)S(1)} %all_to_all.44.p_mat, f32[64,16,128]{2,1,0:T(8,128)S(1)} %all_to_all.46.both), custom_call_target="tpu_custom_call" | custom-call | flops 100000000 | bytes 4915200 | tf_op jit(solution)/shard_map/pallas_call | solution.py:151
  (1 shorter events, 0.0 us)
Async XLA Ops:
  0.6 1.2 copy-start
  1.8 1.2 copy-start.2
  3.0 1.0 copy-start.4
  7.4 56.3 %copy-start.3 = (bf16[1,512,896]{2,1,0:T(8,128)(2,1)S(1)}, bf16[1,512,896]{2,1,0:T(8,128)(2,1)}, u32[]{:S(2)}) copy-start(bf16[1,512,896]{2,1,0:T(8,128)(2,1)} %error.9) | copy-start | bytes 2752516
  7.4 56.3 %copy-start.1 = (bf16[1,512,896]{2,1,0:T(8,128)(2,1)S(1)}, bf16[1,512,896]{2,1,0:T(8,128)(2,1)}, u32[]{:S(2)}) copy-start(bf16[1,512,896]{2,1,0:T(8,128)(2,1)} %grad.9) | copy-start | bytes 2752516
  117.2 22.5 %all-to-all-start.4 = ((f32[64,8,128]{2,1,0:T(8,128)}), f32[64,8,128]{2,1,0:T(8,128)S(1)}, u32[]{:S(2)}, u32[]{:S(2)}) async-start(f32[64,8,128]{2,1,0:T(8,128)} %bitcast.3), calls=%async_computation.4 | async-start | bytes 524288 | tf_op jit(solution)/shard_map/all_to_all | solution.py:169
where the time goes:
time: 211 us
  blocking collectives  171 us (81%)
  Pallas kernels  17.1 us (8%)
  waiting for transfers between devices  10.1 us (5%)
  starting transfers between devices  7.91 us (4%)
  local copies, waits for them, and re-layouts  3.38 us (2%)
    all_to_all x7, blocking collectives, exchange(): return lax.all_to_all(x, axes, 0, 0, tiled=True)  167 us
    pallas_call x10, Pallas kernels, call(): pl.pallas_call(kernel, out_shape=shapes, in_specs=[pl.BlockSpec(memory_sp...  17.1 us
    all_to_all x1, waiting for transfers between devices, exchange(): return lax.all_to_all(x, axes, 0, 0, tiled=True)  10.1 us
    all_to_all x1, starting transfers between devices, exchange(): return lax.all_to_all(x, axes, 0, 0, tiled=True)  7.91 us
    all_gather x2, blocking collectives, left_pieces(): chip = lax.all_gather(partial, 'core').sum(axis=0)  4.36 us
  transfers between devices with their start and end apart: 1, of which 1 were waited for; matrix products, arithmetic and copies ran while one was open for 0% of the time, Pallas kernels for 2%

commit v1 on v0

--- a/solution.py
+++ b/solution.py
@@ -10,7 +10,11 @@
 
 HIGHEST = lax.Precision.HIGHEST
 BLOCK = 32
+CHUNKS = 4
 VMEM_LIMIT = 24 * 2**20
+VMEM_MOST = 64 * 2**20 - 400 * 2**10
+VMEM = pl.BlockSpec(memory_space=pltpu.VMEM)
+HBM = pl.BlockSpec(memory_space=pltpu.HBM)
 
 
 def mm(a, b, on_a, on_b):
@@ -33,6 +37,15 @@
     second = rest.astype(jnp.bfloat16)
     third = (rest - second.astype(jnp.float32)).astype(jnp.bfloat16)
     return first, second, third
+
+
+def mm_wide(a, b):
+    a, b = three_parts(a), three_parts(b)
+    wide_a = jnp.concatenate([a[i] for i in (0, 0, 1, 0, 2, 1)], axis=1)
+    wide_b = jnp.concatenate([b[i] for i in (0, 1, 0, 2, 0, 1)], axis=1)
+    return lax.dot_general(
+        wide_a, wide_b, (((1,), (1,)), ((), ())), preferred_element_type=jnp.float32
+    )
 
 
 def add_parts(x, axis):
@@ -93,8 +106,23 @@
     return add_parts(mm16(grad, parts) + mm16(error, parts), 1) * scale
 
 
-def first_left_kernel(scale, grad, error, q_mat, out):
-    out[...] = left_product(grad[0], error[0], q_mat[...], scale)
+def first_left_kernel(scale, grad, error, q_mat, out, held, q_held, sems, q_sem):
+    rows = held.shape[2]
+    q_copy = pltpu.make_async_copy(q_mat, q_held, q_sem)
+    q_copy.start()
+    copies = []
+    for i in range(CHUNKS):
+        for k, source in enumerate((grad, error)):
+            chunk = source.at[0, pl.ds(i * rows, rows), :]
+            copies.append(pltpu.make_async_copy(chunk, held.at[i, k], sems.at[i, k]))
+            copies[-1].start()
+    q_copy.wait()
+    parts = jnp.concatenate(three_parts(q_held[...]), axis=1)
+    for i in range(CHUNKS):
+        copies[2 * i].wait()
+        copies[2 * i + 1].wait()
+        product = mm16(held[i].reshape(2 * rows, -1), parts)
+        out[pl.ds(i * rows, rows), :] = add_parts(product[:rows] + product[rows:], 1) * scale
 
 
 def next_left_kernel(scale, grad, error, both, out):
@@ -105,7 +133,7 @@
 
 
 def right_kernel(scale, grad, error, p_mat, out):
-    p_mat = p_mat[...].reshape(-1, p_mat.shape[2])
+    p_mat = p_mat[...]
     p_t = p_mat.T
     parts = jnp.concatenate(three_parts(p_t), axis=0)
     term = add_parts(mm16(parts, grad[0]) + mm16(parts, error[0]), 0).T
@@ -131,34 +159,48 @@
     out[...] = lower_inverse(gram * by_row * by_lane)
 
 
-def last_kernel(grad, error, p_mat, both, new_error, q_factor):
+def core_half_kernel(partials, out):
+    rows = out.shape[0]
+    start = pl.multiple_of(lax.axis_index("core") * rows, rows)
+    out[...] = partials[0, pl.ds(start, rows), :] + partials[1, pl.ds(start, rows), :]
+
+
+def last_kernel(grad, error, p_mat, both, new_error, q_factor, held, q_held, sems, q_sem):
     cols = grad.shape[2]
-    p_mat = p_mat[...].reshape(-1, p_mat.shape[2])
     both = both[...].reshape(-1, both.shape[2])
     inverse = lower_inverse(both[cols:])
-    q_mat = mm(both[:cols], inverse, 1, 1)
-    q_factor[...] = q_mat
-    p_hat = mm(p_mat, inverse, 1, 1)
-    approx = mm(p_hat, q_mat, 1, 1)
-    comp = grad[0].astype(jnp.float32) + error[0].astype(jnp.float32)
-    new_error[0] = (comp - approx).astype(jnp.bfloat16)
-
-
-def call(kernel, shapes, *operands, flops=10**8):
+    q_mat = mm_wide(both[:cols], inverse)
+    q_held[...] = q_mat
+    copies = [pltpu.make_async_copy(q_held, q_factor, q_sem)]
+    copies[0].start()
+    p_hat = mm_wide(p_mat[...], inverse)
+    rows = held.shape[1] // CHUNKS
+    for i in range(CHUNKS):
+        part = pl.ds(i * rows, rows)
+        comp = grad[0, part, :].astype(jnp.float32) + error[0, part, :].astype(jnp.float32)
+        approx = mm_wide(p_hat[i * rows : (i + 1) * rows], q_mat)
+        held[0, part, :] = (comp - approx).astype(jnp.bfloat16)
+        chunk = new_error.at[0, part, :]
+        copies.append(pltpu.make_async_copy(held.at[0, part, :], chunk, sems.at[i]))
+        copies[-1].start()
+    for copy in copies:
+        copy.wait()
+
+
+def call(kernel, shapes, *operands, flops=10**8, **more):
     n_bytes = sum(x.size * x.dtype.itemsize for x in operands)
-    single = not isinstance(shapes, tuple)
-    outs = (shapes,) if single else shapes
-    result = pl.pallas_call(
+    n_bytes += sum(s.size * s.dtype.itemsize for s in jax.tree.leaves(shapes))
+    return pl.pallas_call(
         kernel,
         out_shape=shapes,
-        in_specs=[pl.BlockSpec(memory_space=pltpu.VMEM)] * len(operands),
-        out_specs=jax.tree.map(lambda _: pl.BlockSpec(memory_space=pltpu.VMEM), shapes),
-        compiler_params=pltpu.CompilerParams(vmem_limit_bytes=VMEM_LIMIT),
-        cost_estimate=pl.CostEstimate(
-            flops=flops, bytes_accessed=n_bytes + sum(s.size * 4 for s in outs), transcendentals=0
+        in_specs=more.pop("in_specs", [VMEM] * len(operands)),
+        out_specs=more.pop("out_specs", VMEM),
+        compiler_params=pltpu.CompilerParams(
+            vmem_limit_bytes=more.pop("vmem_limit_bytes", VMEM_LIMIT)
         ),
+        cost_estimate=pl.CostEstimate(flops=flops, bytes_accessed=n_bytes, transcendentals=0),
+        **more,
     )(*operands)
-    return result
 
 
 def f32(*shape):
@@ -175,12 +217,18 @@
     scale = 1.0 / lax.axis_size("dp")
     left_axes, right_axes = ("dp", "y"), ("dp", "row")
     n_left, n_right = lax.axis_size(left_axes), lax.axis_size(right_axes)
-    left_shape = f32(n_left, rows // n_left, rank)
+    half = rows // lax.axis_size("core")
+    left_shape = f32(n_left, half // n_left, rank)
     right_shape = f32(n_right, (cols + rank) // n_right, rank)
+    chunk = rows // CHUNKS
 
     def left_pieces(partial):
-        chip = lax.all_gather(partial, "core").sum(axis=0)
+        chip = call(core_half_kernel, f32(half, rank), lax.all_gather(partial, "core"))
         return exchange(chip.reshape(left_shape.shape), left_axes)
+
+    def left_gathered(pieces):
+        mine = exchange(pieces, left_axes).reshape(half, rank)
+        return lax.all_gather(mine, "core", tiled=True)
 
     def right_total(p_all):
         partial = call(functools.partial(right_kernel, scale), right_shape, grad, error, p_all)
@@ -188,15 +236,27 @@
         return exchange(call(sum_kernel, right_shape, pieces), right_axes)
 
     partial = call(
-        functools.partial(first_left_kernel, scale), f32(rows, rank), grad, error, q_init
+        functools.partial(first_left_kernel, scale),
+        f32(rows, rank),
+        grad,
+        error,
+        q_init,
+        in_specs=[HBM] * 3,
+        vmem_limit_bytes=VMEM_MOST,
+        scratch_shapes=[
+            pltpu.VMEM((CHUNKS, 2, chunk, cols), jnp.bfloat16),
+            pltpu.VMEM((cols, rank), jnp.float32),
+            pltpu.SemaphoreType.DMA((CHUNKS, 2)),
+            pltpu.SemaphoreType.DMA,
+        ],
     )
     pieces = left_pieces(partial)
-    p_all = exchange(call(sum_kernel, left_shape, pieces), left_axes)
+    p_all = left_gathered(call(sum_kernel, left_shape, pieces))
     both = right_total(p_all)
     partial = call(functools.partial(next_left_kernel, scale), f32(rows, rank), grad, error, both)
     inverse = call(inverse_kernel, f32(rank, rank), both, flops=4 * 10**9)
     pieces = left_pieces(partial)
-    p_all = exchange(call(sum_scale_kernel, left_shape, pieces, inverse), left_axes)
+    p_all = left_gathered(call(sum_scale_kernel, left_shape, pieces, inverse))
     both = right_total(p_all)
     return call(
         last_kernel,
@@ -205,6 +265,13 @@
         error,
         p_all,
         both,
+        out_specs=(HBM, HBM),
+        scratch_shapes=[
+            pltpu.VMEM((1, rows, cols), jnp.bfloat16),
+            pltpu.VMEM((cols, rank), jnp.float32),
+            pltpu.SemaphoreType.DMA((CHUNKS,)),
+            pltpu.SemaphoreType.DMA,
+        ],
     )
 
 

time: 211 us -> 214 us (1.014)
  the two profiles are of different devices: /device:TPU:16 before, /device:TPU:1 now
where the time goes in v1:
time: 214 us; the launch traced here: 211 us
  blocking collectives  178 us (83%)
  Pallas kernels  20.7 us (10%)
  waiting for transfers between devices  7.03 us (3%)
  starting transfers between devices  4.62 us (2%)
    all_to_all x7, blocking collectives, exchange(): return lax.all_to_all(x, axes, 0, 0, tiled=True)  148 us
    all_gather x2, blocking collectives, left_pieces(): lax.all_gather(partial, 'core')  22.1 us
    pallas_call x12, Pallas kernels, call(): pl.pallas_call(kernel, out_shape=shapes, in_specs=more.pop('in_specs', [V...  20.7 us
    all_gather x2, blocking collectives, left_gathered(): return lax.all_gather(mine, 'core', tiled=True)  8.22 us
    all_to_all x1, waiting for transfers between devices, exchange(): return lax.all_to_all(x, axes, 0, 0, tiled=True)  7.03 us
    all_to_all x1, starting transfers between devices, exchange(): return lax.all_to_all(x, axes, 0, 0, tiled=True)  4.62 us
  transfers between devices with their start and end apart: 1, of which 1 were waited for; matrix products, arithmetic and copies ran while one was open for 0% of the time, Pallas kernels for 2%

profile of v1, /device:TPU:1, one launch (start us, length us, event | category | flops | bytes accessed | tf_op | source)
XLA Modules:
  0.0 211.1 jit_solution(16250132177603016721)
XLA Ops:
  0.6 4.3 %shard_map.50 = f32[512,128]{1,0:T(8,128)} custom-call(bf16[1,512,896]{2,1,0:T(8,128)(2,1)} %grad.9, bf16[1,512,896]{2,1,0:T(8,128)(2,1)} %error.9, f32[896,128]{1,0:T(8,128)} %q_mat.1), custom_call_target="tpu_custom_call" | custom-call | flops 100000000 | bytes 2555904 | tf_op jit(solution)/shard_map/pallas_call | solution.py:193
  4.9 16.2 %all-gather = f32[1024,128]{1,0:T(8,128)S(1)} all-gather(f32[512,128]{1,0:T(8,128)} %shard_map.50), channel_id=2, replica_groups=mesh['dp'=8,'row'=8,'y'=8,'core'=2] {'core'}, dimensions={0}, use_global_device_ids=true | all-gather | bytes 786432 | tf_op jit(solution)/shard_map/all_gather | solution.py:226
  21.1 0.0 copy-start
  21.1 0.0 copy-start.1
  21.1 21.9 %all_to_all.40.pieces = f32[64,4,128]{2,1,0:T(4,128)S(1)} all-to-all(f32[64,4,128]{2,1,0:T(4,128)S(1)} %bitcast.8), channel_id=1, replica_groups=mesh['dp'=8,'row'=8,'y'=8,'core'=2] {'dp','y'}, dimensions={0} | all-to-all | bytes 262144 | tf_op jit(solution)/shard_map/all_to_all | solution.py:211
  43.1 0.1 shard_map.52
  43.2 15.8 %all_to_all.41 = f32[64,4,128]{2,1,0:T(4,128)S(1)} all-to-all(f32[64,4,128]{2,1,0:T(4,128)S(1)} %shard_map.52), channel_id=1, replica_groups=mesh['dp'=8,'row'=8,'y'=8,'core'=2] {'dp','y'}, dimensions={0} | all-to-all | bytes 262144 | tf_op jit(solution)/shard_map/all_to_all | solution.py:211
  58.9 4.4 %all_gather.20.p_mat = f32[512,128]{1,0:T(8,128)S(1)} all-gather(f32[256,128]{1,0:T(8,128)S(1)} %bitcast.9), channel_id=1, replica_groups=mesh['dp'=8,'row'=8,'y'=8,'core'=2] {'core'}, dimensions={0}, use_global_device_ids=true | all-gather | bytes 393216 | tf_op jit(solution)/shard_map/all_gather | solution.py:231
  63.3 0.0 copy-done
  63.3 0.0 copy-done.1
  63.3 1.2 shard_map.53
  64.6 25.3 %all_to_all.42.pieces = f32[64,16,128]{2,1,0:T(8,128)S(1)} all-to-all(f32[64,16,128]{2,1,0:T(8,128)S(1)} %shard_map.53), channel_id=1, replica_groups=mesh['dp'=8,'row'=8,'y'=8,'core'=2] {'dp','row'}, dimensions={0} | all-to-all | bytes 1048576 | tf_op jit(solution)/shard_map/all_to_all | solution.py:211
  89.9 0.1 shard_map.54
  90.0 22.9 %all_to_all.43.both = f32[64,16,128]{2,1,0:T(8,128)S(1)} all-to-all(f32[64,16,128]{2,1,0:T(8,128)S(1)} %shard_map.54), channel_id=1, replica_groups=mesh['dp'=8,'row'=8,'y'=8,'core'=2] {'dp','row'}, dimensions={0} | all-to-all | bytes 1048576 | tf_op jit(solution)/shard_map/all_to_all | solution.py:211
  112.9 1.2 shard_map.55
  114.1 6.0 %all-gather.1 = f32[1024,128]{1,0:T(8,128)S(1)} all-gather(f32[512,128]{1,0:T(8,128)S(1)} %shard_map.55), channel_id=3, replica_groups=mesh['dp'=8,'row'=8,'y'=8,'core'=2] {'core'}, dimensions={0}, use_global_device_ids=true | all-gather | bytes 786432 | tf_op jit(solution)/shard_map/all_gather | solution.py:226
  120.0 0.7 shard_map.56
  120.7 4.6 %all-to-all-start.4 = ((f32[64,4,128]{2,1,0:T(4,128)}), f32[64,4,128]{2,1,0:T(4,128)S(1)}, u32[]{:S(2)}, u32[]{:S(2)}) async-start(f32[64,4,128]{2,1,0:T(4,128)} %bitcast.4), calls=%async_computation.4 | async-start | bytes 262144 | tf_op jit(solution)/shard_map/all_to_all | solution.py:211
  125.3 4.5 %shard_map.57.inverse = f32[128,128]{1,0:T(8,128)S(1)} custom-call(f32[64,16,128]{2,1,0:T(8,128)S(1)} %all_to_all.43.both), custom_call_target="tpu_custom_call" | custom-call | flops 4000000000 | bytes 589824 | tf_op jit(solution)/shard_map/pallas_call | solution.py:193
  129.9 7.0 %all-to-all-done.4.pieces = f32[64,4,128]{2,1,0:T(4,128)S(1)} async-done(((f32[64,4,128]{2,1,0:T(4,128)}), f32[64,4,128]{2,1,0:T(4,128)S(1)}, u32[]{:S(2)}, u32[]{:S(2)}) %all-to-all-start.4) | async-done | bytes 131104 | tf_op jit(solution)/shard_map/all_to_all | solution.py:211
  136.9 0.3 shard_map.58
  137.2 16.5 %all_to_all.44 = f32[64,4,128]{2,1,0:T(4,128)S(1)} all-to-all(f32[64,4,128]{2,1,0:T(4,128)S(1)} %shard_map.58), channel_id=1, replica_groups=mesh['dp'=8,'row'=8,'y'=8,'core'=2] {'dp','y'}, dimensions={0} | all-to-all | bytes 262144 | tf_op jit(solution)/shard_map/all_to_all | solution.py:211
  153.7 3.8 %all_gather.23.p_mat = f32[512,128]{1,0:T(8,128)S(1)} all-gather(f32[256,128]{1,0:T(8,128)S(1)} %bitcast.10), channel_id=1, replica_groups=mesh['dp'=8,'row'=8,'y'=8,'core'=2] {'core'}, dimensions={0}, use_global_device_ids=true | all-gather | bytes 393216 | tf_op jit(solution)/shard_map/all_gather | solution.py:231
  157.5 1.2 shard_map.59
  158.7 22.4 %all_to_all.45.pieces = f32[64,16,128]{2,1,0:T(8,128)S(1)} all-to-all(f32[64,16,128]{2,1,0:T(8,128)S(1)} %shard_map.59), channel_id=1, replica_groups=mesh['dp'=8,'row'=8,'y'=8,'core'=2] {'dp','row'}, dimensions={0} | all-to-all | bytes 1048576 | tf_op jit(solution)/shard_map/all_to_all | solution.py:211
  181.1 0.1 shard_map.60
  181.2 22.9 %all_to_all.46.both = f32[64,16,128]{2,1,0:T(8,128)S(1)} all-to-all(f32[64,16,128]{2,1,0:T(8,128)S(1)} %shard_map.60), channel_id=1, replica_groups=mesh['dp'=8,'row'=8,'y'=8,'core'=2] {'dp','row'}, dimensions={0} | all-to-all | bytes 1048576 | tf_op jit(solution)/shard_map/all_to_all | solution.py:211
  204.1 6.9 %shard_map.61 = (bf16[1,512,896]{2,1,0:T(8,128)(2,1)}, f32[896,128]{1,0:T(8,128)}) custom-call(bf16[1,512,896]{2,1,0:T(8,128)(2,1)S(1)} %copy-done, bf16[1,512,896]{2,1,0:T(8,128)(2,1)S(1)} %copy-done.1, f32[512,128]{1,0:T(8,128)S(1)} %all_gather.23.p_mat, f32[64,16,128]{2,1,0:T(8,128)S(1)} %all_to_all.46.both), custom_call_target="tpu_custom_call" | custom-call | flops 100000000 | bytes 3997696 | tf_op jit(solution)/shard_map/pallas_call | solution.py:193
  (1 shorter events, 0.0 us)
Async XLA Ops:
  21.1 42.2 %copy-start = (bf16[1,512,896]{2,1,0:T(8,128)(2,1)S(1)}, bf16[1,512,896]{2,1,0:T(8,128)(2,1)}, u32[]{:S(2)}) copy-start(bf16[1,512,896]{2,1,0:T(8,128)(2,1)} %grad.9) | copy-start | bytes 2752516
  21.1 42.2 %copy-start.1 = (bf16[1,512,896]{2,1,0:T(8,128)(2,1)S(1)}, bf16[1,512,896]{2,1,0:T(8,128)(2,1)}, u32[]{:S(2)}) copy-start(bf16[1,512,896]{2,1,0:T(8,128)(2,1)} %error.9) | copy-start | bytes 2752516
  120.7 16.2 %all-to-all-start.4 = ((f32[64,4,128]{2,1,0:T(4,128)}), f32[64,4,128]{2,1,0:T(4,128)S(1)}, u32[]{:S(2)}, u32[]{:S(2)}) async-start(f32[64,4,128]{2,1,0:T(4,128)} %bitcast.4), calls=%async_computation.4 | async-start | bytes 262144 | tf_op jit(solution)/shard_map/all_to_all | solution.py:211

commit v2 on v1

--- a/solution.py
+++ b/solution.py
@@ -10,9 +10,9 @@
 
 HIGHEST = lax.Precision.HIGHEST
 BLOCK = 32
-CHUNKS = 4
+CHUNKS = 2
 VMEM_LIMIT = 24 * 2**20
-VMEM_MOST = 64 * 2**20 - 400 * 2**10
+VMEM_MOST = 64 * 2**20 - 440 * 2**10
 VMEM = pl.BlockSpec(memory_space=pltpu.VMEM)
 HBM = pl.BlockSpec(memory_space=pltpu.HBM)
 
@@ -107,22 +107,17 @@
 
 
 def first_left_kernel(scale, grad, error, q_mat, out, held, q_held, sems, q_sem):
-    rows = held.shape[2]
-    q_copy = pltpu.make_async_copy(q_mat, q_held, q_sem)
-    q_copy.start()
-    copies = []
-    for i in range(CHUNKS):
-        for k, source in enumerate((grad, error)):
-            chunk = source.at[0, pl.ds(i * rows, rows), :]
-            copies.append(pltpu.make_async_copy(chunk, held.at[i, k], sems.at[i, k]))
-            copies[-1].start()
-    q_copy.wait()
+    copies = [pltpu.make_async_copy(q_mat, q_held, q_sem)]
+    for k, source in enumerate((grad, error)):
+        copies.append(pltpu.make_async_copy(source.at[0], held.at[k], sems.at[k]))
+    for copy in copies:
+        copy.start()
+    copies[0].wait()
     parts = jnp.concatenate(three_parts(q_held[...]), axis=1)
-    for i in range(CHUNKS):
-        copies[2 * i].wait()
-        copies[2 * i + 1].wait()
-        product = mm16(held[i].reshape(2 * rows, -1), parts)
-        out[pl.ds(i * rows, rows), :] = add_parts(product[:rows] + product[rows:], 1) * scale
+    copies[1].wait()
+    product = mm16(held[0], parts)
+    copies[2].wait()
+    out[...] = add_parts(product + mm16(held[1], parts), 1) * scale
 
 
 def next_left_kernel(scale, grad, error, both, out):
@@ -133,7 +128,7 @@
 
 
 def right_kernel(scale, grad, error, p_mat, out):
-    p_mat = p_mat[...]
+    p_mat = p_mat[...].reshape(-1, p_mat.shape[2])
     p_t = p_mat.T
     parts = jnp.concatenate(three_parts(p_t), axis=0)
     term = add_parts(mm16(parts, grad[0]) + mm16(parts, error[0]), 0).T
@@ -159,10 +154,8 @@
     out[...] = lower_inverse(gram * by_row * by_lane)
 
 
-def core_half_kernel(partials, out):
-    rows = out.shape[0]
-    start = pl.multiple_of(lax.axis_index("core") * rows, rows)
-    out[...] = partials[0, pl.ds(start, rows), :] + partials[1, pl.ds(start, rows), :]
+def core_sum_kernel(partials, out):
+    out[...] = (partials[0] + partials[1]).reshape(out.shape)
 
 
 def last_kernel(grad, error, p_mat, both, new_error, q_factor, held, q_held, sems, q_sem):
@@ -173,7 +166,7 @@
     q_held[...] = q_mat
     copies = [pltpu.make_async_copy(q_held, q_factor, q_sem)]
     copies[0].start()
-    p_hat = mm_wide(p_mat[...], inverse)
+    p_hat = mm_wide(p_mat[...].reshape(-1, p_mat.shape[2]), inverse)
     rows = held.shape[1] // CHUNKS
     for i in range(CHUNKS):
         part = pl.ds(i * rows, rows)
@@ -217,18 +210,12 @@
     scale = 1.0 / lax.axis_size("dp")
     left_axes, right_axes = ("dp", "y"), ("dp", "row")
     n_left, n_right = lax.axis_size(left_axes), lax.axis_size(right_axes)
-    half = rows // lax.axis_size("core")
-    left_shape = f32(n_left, half // n_left, rank)
+    left_shape = f32(n_left, rows // n_left, rank)
     right_shape = f32(n_right, (cols + rank) // n_right, rank)
-    chunk = rows // CHUNKS
 
     def left_pieces(partial):
-        chip = call(core_half_kernel, f32(half, rank), lax.all_gather(partial, "core"))
-        return exchange(chip.reshape(left_shape.shape), left_axes)
-
-    def left_gathered(pieces):
-        mine = exchange(pieces, left_axes).reshape(half, rank)
-        return lax.all_gather(mine, "core", tiled=True)
+        chip = call(core_sum_kernel, left_shape, lax.all_gather(partial, "core"))
+        return exchange(chip, left_axes)
 
     def right_total(p_all):
         partial = call(functools.partial(right_kernel, scale), right_shape, grad, error, p_all)
@@ -244,19 +231,19 @@
         in_specs=[HBM] * 3,
         vmem_limit_bytes=VMEM_MOST,
         scratch_shapes=[
-            pltpu.VMEM((CHUNKS, 2, chunk, cols), jnp.bfloat16),
+            pltpu.VMEM((2, rows, cols), jnp.bfloat16),
             pltpu.VMEM((cols, rank), jnp.float32),
-            pltpu.SemaphoreType.DMA((CHUNKS, 2)),
+            pltpu.SemaphoreType.DMA((2,)),
             pltpu.SemaphoreType.DMA,
         ],
     )
     pieces = left_pieces(partial)
-    p_all = left_gathered(call(sum_kernel, left_shape, pieces))
+    p_all = exchange(call(sum_kernel, left_shape, pieces), left_axes)
     both = right_total(p_all)
     partial = call(functools.partial(next_left_kernel, scale), f32(rows, rank), grad, error, both)
     inverse = call(inverse_kernel, f32(rank, rank), both, flops=4 * 10**9)
     pieces = left_pieces(partial)
-    p_all = left_gathered(call(sum_scale_kernel, left_shape, pieces, inverse))
+    p_all = exchange(call(sum_scale_kernel, left_shape, pieces, inverse), left_axes)
     both = right_total(p_all)
     return call(
         last_kernel,

time: 214 us -> 209 us (0.977)
  the two profiles are of different devices: /device:TPU:1 before, /device:TPU:16 now
where the time goes in v2:
time: 209 us
  blocking collectives  171 us (82%)
  Pallas kernels  19.4 us (9%)
  waiting for transfers between devices  10.1 us (5%)
  starting transfers between devices  7.9 us (4%)
    all_to_all x7, blocking collectives, exchange(): return lax.all_to_all(x, axes, 0, 0, tiled=True)  166 us
    pallas_call x12, Pallas kernels, call(): pl.pallas_call(kernel, out_shape=shapes, in_specs=more.pop('in_specs', [V...  19.4 us
    all_to_all x1, waiting for transfers between devices, exchange(): return lax.all_to_all(x, axes, 0, 0, tiled=True)  10.1 us
    all_to_all x1, starting transfers between devices, exchange(): return lax.all_to_all(x, axes, 0, 0, tiled=True)  7.9 us
    all_gather x2, blocking collectives, left_pieces(): chip = call(core_sum_kernel, left_shape, lax.all_gather(partial, 'core'))  4.57 us
  transfers between devices with their start and end apart: 1, of which 1 were waited for; matrix products, arithmetic and copies ran while one was open for 0% of the time, Pallas kernels for 2%

profile of v2, /device:TPU:16, one launch (start us, length us, event | category | flops | bytes accessed | tf_op | source)
XLA Modules:
  0.0 209.0 jit_solution(15942679345110929563)
XLA Ops:
  0.6 3.5 %shard_map.50 = f32[512,128]{1,0:T(8,128)} custom-call(bf16[1,512,896]{2,1,0:T(8,128)(2,1)} %grad.9, bf16[1,512,896]{2,1,0:T(8,128)(2,1)} %error.9, f32[896,128]{1,0:T(8,128)} %q_mat.1), custom_call_target="tpu_custom_call" | custom-call | flops 100000000 | bytes 2555904 | tf_op jit(solution)/shard_map/pallas_call | solution.py:186
  4.1 2.4 %all-gather = f32[1024,128]{1,0:T(8,128)S(1)} all-gather(f32[512,128]{1,0:T(8,128)} %shard_map.50), channel_id=2, replica_groups=mesh['dp'=8,'row'=8,'y'=8,'core'=2] {'core'}, dimensions={0}, use_global_device_ids=true | all-gather | bytes 786432 | tf_op jit(solution)/shard_map/all_gather | solution.py:217
  6.5 0.0 copy-start.1
  6.6 0.0 copy-start
  6.6 37.8 %all_to_all.40.pieces = f32[64,8,128]{2,1,0:T(8,128)S(1)} all-to-all(f32[64,8,128]{2,1,0:T(8,128)S(1)} %shard_map.51), channel_id=1, replica_groups=mesh['dp'=8,'row'=8,'y'=8,'core'=2] {'dp','y'}, dimensions={0} | all-to-all | bytes 524288 | tf_op jit(solution)/shard_map/all_to_all | solution.py:204
  44.4 0.1 shard_map.52
  44.5 18.3 %all_to_all.41.p_mat = f32[64,8,128]{2,1,0:T(8,128)S(1)} all-to-all(f32[64,8,128]{2,1,0:T(8,128)S(1)} %shard_map.52), channel_id=1, replica_groups=mesh['dp'=8,'row'=8,'y'=8,'core'=2] {'dp','y'}, dimensions={0} | all-to-all | bytes 524288 | tf_op jit(solution)/shard_map/all_to_all | solution.py:204
  62.9 0.0 copy-done.1
  62.9 0.0 copy-done
  62.9 1.2 shard_map.53
  64.1 26.0 %all_to_all.42.pieces = f32[64,16,128]{2,1,0:T(8,128)S(1)} all-to-all(f32[64,16,128]{2,1,0:T(8,128)S(1)} %shard_map.53), channel_id=1, replica_groups=mesh['dp'=8,'row'=8,'y'=8,'core'=2] {'dp','row'}, dimensions={0} | all-to-all | bytes 1048576 | tf_op jit(solution)/shard_map/all_to_all | solution.py:204
  90.1 0.1 shard_map.54
  90.2 21.9 %all_to_all.43.both = f32[64,16,128]{2,1,0:T(8,128)S(1)} all-to-all(f32[64,16,128]{2,1,0:T(8,128)S(1)} %shard_map.54), channel_id=1, replica_groups=mesh['dp'=8,'row'=8,'y'=8,'core'=2] {'dp','row'}, dimensions={0} | all-to-all | bytes 1048576 | tf_op jit(solution)/shard_map/all_to_all | solution.py:204
  112.2 1.2 shard_map.55
  113.4 2.2 %all-gather.1 = f32[1024,128]{1,0:T(8,128)S(1)} all-gather(f32[512,128]{1,0:T(8,128)S(1)} %shard_map.55), channel_id=3, replica_groups=mesh['dp'=8,'row'=8,'y'=8,'core'=2] {'core'}, dimensions={0}, use_global_device_ids=true | all-gather | bytes 786432 | tf_op jit(solution)/shard_map/all_gather | solution.py:217
  115.6 0.7 shard_map.56
  116.3 7.9 %all-to-all-start.4 = ((f32[64,8,128]{2,1,0:T(8,128)}), f32[64,8,128]{2,1,0:T(8,128)S(1)}, u32[]{:S(2)}, u32[]{:S(2)}) async-start(f32[64,8,128]{2,1,0:T(8,128)} %shard_map.56), calls=%async_computation.4 | async-start | bytes 524288 | tf_op jit(solution)/shard_map/all_to_all | solution.py:204
  124.2 4.5 %shard_map.57.inverse = f32[128,128]{1,0:T(8,128)S(1)} custom-call(f32[64,16,128]{2,1,0:T(8,128)S(1)} %all_to_all.43.both), custom_call_target="tpu_custom_call" | custom-call | flops 4000000000 | bytes 589824 | tf_op jit(solution)/shard_map/pallas_call | solution.py:186
  128.8 10.1 %all-to-all-done.4.pieces = f32[64,8,128]{2,1,0:T(8,128)S(1)} async-done(((f32[64,8,128]{2,1,0:T(8,128)}), f32[64,8,128]{2,1,0:T(8,128)S(1)}, u32[]{:S(2)}, u32[]{:S(2)}) %all-to-all-start.4) | async-done | bytes 262176 | tf_op jit(solution)/shard_map/all_to_all | solution.py:204
  138.8 0.3 shard_map.58
  139.1 18.4 %all_to_all.44.p_mat = f32[64,8,128]{2,1,0:T(8,128)S(1)} all-to-all(f32[64,8,128]{2,1,0:T(8,128)S(1)} %shard_map.58), channel_id=1, replica_groups=mesh['dp'=8,'row'=8,'y'=8,'core'=2] {'dp','y'}, dimensions={0} | all-to-all | bytes 524288 | tf_op jit(solution)/shard_map/all_to_all | solution.py:204
  157.5 1.2 shard_map.59
  158.8 21.7 %all_to_all.45.pieces = f32[64,16,128]{2,1,0:T(8,128)S(1)} all-to-all(f32[64,16,128]{2,1,0:T(8,128)S(1)} %shard_map.59), channel_id=1, replica_groups=mesh['dp'=8,'row'=8,'y'=8,'core'=2] {'dp','row'}, dimensions={0} | all-to-all | bytes 1048576 | tf_op jit(solution)/shard_map/all_to_all | solution.py:204
  180.4 0.1 shard_map.60
  180.5 21.9 %all_to_all.46.both = f32[64,16,128]{2,1,0:T(8,128)S(1)} all-to-all(f32[64,16,128]{2,1,0:T(8,128)S(1)} %shard_map.60), channel_id=1, replica_groups=mesh['dp'=8,'row'=8,'y'=8,'core'=2] {'dp','row'}, dimensions={0} | all-to-all | bytes 1048576 | tf_op jit(solution)/shard_map/all_to_all | solution.py:204
  202.5 6.4 %shard_map.61 = (bf16[1,512,896]{2,1,0:T(8,128)(2,1)}, f32[896,128]{1,0:T(8,128)}) custom-call(bf16[1,512,896]{2,1,0:T(8,128)(2,1)S(1)} %copy-done, bf16[1,512,896]{2,1,0:T(8,128)(2,1)S(1)} %copy-done.1, f32[64,8,128]{2,1,0:T(8,128)S(1)} %all_to_all.44.p_mat, f32[64,16,128]{2,1,0:T(8,128)S(1)} %all_to_all.46.both), custom_call_target="tpu_custom_call" | custom-call | flops 100000000 | bytes 3997696 | tf_op jit(solution)/shard_map/pallas_call | solution.py:186
  (1 shorter events, 0.0 us)
Async XLA Ops:
  6.5 56.3 %copy-start.1 = (bf16[1,512,896]{2,1,0:T(8,128)(2,1)S(1)}, bf16[1,512,896]{2,1,0:T(8,128)(2,1)}, u32[]{:S(2)}) copy-start(bf16[1,512,896]{2,1,0:T(8,128)(2,1)} %error.9) | copy-start | bytes 2752516
  6.6 56.3 %copy-start = (bf16[1,512,896]{2,1,0:T(8,128)(2,1)S(1)}, bf16[1,512,896]{2,1,0:T(8,128)(2,1)}, u32[]{:S(2)}) copy-start(bf16[1,512,896]{2,1,0:T(8,128)(2,1)} %grad.9) | copy-start | bytes 2752516
  116.3 22.5 %all-to-all-start.4 = ((f32[64,8,128]{2,1,0:T(8,128)}), f32[64,8,128]{2,1,0:T(8,128)S(1)}, u32[]{:S(2)}, u32[]{:S(2)}) async-start(f32[64,8,128]{2,1,0:T(8,128)} %shard_map.56), calls=%async_computation.4 | async-start | bytes 524288 | tf_op jit(solution)/shard_map/all_to_all | solution.py:204

commit v3 on v2

--- a/solution.py
+++ b/solution.py
@@ -120,11 +120,27 @@
     out[...] = add_parts(product + mm16(held[1], parts), 1) * scale
 
 
+def second_core_inverse(gram, out):
+    second = lax.axis_index("core") == 1
+
+    @pl.when(second)
+    def _():
+        out[...] = lower_inverse(gram)
+
+    @pl.when(jnp.logical_not(second))
+    def _():
+        out[...] = jnp.zeros_like(out)
+
+
 def next_left_kernel(scale, grad, error, both, out):
-    cols = grad.shape[2]
+    rows, cols = grad.shape[1:]
     both = both[...].reshape(-1, both.shape[2])
-    q_mat = both[:cols] * lax.rsqrt(diagonal(both[cols:], 0))
-    out[...] = left_product(grad[0], error[0], q_mat, scale)
+    gram = both[cols:]
+    by_lane = lax.rsqrt(diagonal(gram, 0))
+    product = left_product(grad[0], error[0], both[:cols] * by_lane, scale)
+    out[pl.ds(0, rows), :] = product
+    by_row = lax.rsqrt(diagonal(gram, 1))
+    second_core_inverse(gram * by_row * by_lane, out.at[pl.ds(rows, gram.shape[0]), :])
 
 
 def right_kernel(scale, grad, error, p_mat, out):
@@ -148,20 +164,23 @@
 
 def inverse_kernel(both, out):
     n = out.shape[0]
-    gram = both[...].reshape(-1, n)[-n:]
-    by_row = lax.rsqrt(diagonal(gram, 1))
-    by_lane = lax.rsqrt(diagonal(gram, 0))
-    out[...] = lower_inverse(gram * by_row * by_lane)
+    second_core_inverse(both[...].reshape(-1, n)[-n:], out)
 
 
 def core_sum_kernel(partials, out):
     out[...] = (partials[0] + partials[1]).reshape(out.shape)
 
 
-def last_kernel(grad, error, p_mat, both, new_error, q_factor, held, q_held, sems, q_sem):
+def core_sum_inverse_kernel(partials, out, inverse):
+    rows = partials.shape[1] - inverse.shape[0]
+    out[...] = (partials[0, :rows] + partials[1, :rows]).reshape(out.shape)
+    inverse[...] = partials[1, rows:]
+
+
+def last_kernel(grad, error, p_mat, both, inverses, new_error, q_factor, held, q_held, sems, q_sem):
     cols = grad.shape[2]
     both = both[...].reshape(-1, both.shape[2])
-    inverse = lower_inverse(both[cols:])
+    inverse = inverses[1]
     q_mat = mm_wide(both[:cols], inverse)
     q_held[...] = q_mat
     copies = [pltpu.make_async_copy(q_held, q_factor, q_sem)]
@@ -213,10 +232,6 @@
     left_shape = f32(n_left, rows // n_left, rank)
     right_shape = f32(n_right, (cols + rank) // n_right, rank)
 
-    def left_pieces(partial):
-        chip = call(core_sum_kernel, left_shape, lax.all_gather(partial, "core"))
-        return exchange(chip, left_axes)
-
     def right_total(p_all):
         partial = call(functools.partial(right_kernel, scale), right_shape, grad, error, p_all)
         pieces = exchange(partial, right_axes)
@@ -237,14 +252,23 @@
             pltpu.SemaphoreType.DMA,
         ],
     )
-    pieces = left_pieces(partial)
+    chip = call(core_sum_kernel, left_shape, lax.all_gather(partial, "core"))
+    pieces = exchange(chip, left_axes)
     p_all = exchange(call(sum_kernel, left_shape, pieces), left_axes)
     both = right_total(p_all)
-    partial = call(functools.partial(next_left_kernel, scale), f32(rows, rank), grad, error, both)
-    inverse = call(inverse_kernel, f32(rank, rank), both, flops=4 * 10**9)
-    pieces = left_pieces(partial)
+    partial = call(
+        functools.partial(next_left_kernel, scale), f32(rows + rank, rank), grad, error, both
+    )
+    chip, inverse = call(
+        core_sum_inverse_kernel,
+        (left_shape, f32(rank, rank)),
+        lax.all_gather(partial, "core"),
+        out_specs=(VMEM, VMEM),
+    )
+    pieces = exchange(chip, left_axes)
     p_all = exchange(call(sum_scale_kernel, left_shape, pieces, inverse), left_axes)
     both = right_total(p_all)
+    inverses = lax.all_gather(call(inverse_kernel, f32(rank, rank), both), "core")
     return call(
         last_kernel,
         (jax.ShapeDtypeStruct(grad.shape, jnp.bfloat16), f32(cols, rank)),
@@ -252,6 +276,7 @@
         error,
         p_all,
         both,
+        inverses,
         out_specs=(HBM, HBM),
         scratch_shapes=[
             pltpu.VMEM((1, rows, cols), jnp.bfloat16),

time: 209 us -> 210 us (level)
  the two profiles are of different devices: /device:TPU:16 before, /device:TPU:1 now
where the time goes in v3:
time: 210 us
  blocking collectives  191 us (91%)
  Pallas kernels  17.9 us (9%)
    all_to_all x8, blocking collectives, exchange(): return lax.all_to_all(x, axes, 0, 0, tiled=True)  167 us
    pallas_call x12, Pallas kernels, call(): pl.pallas_call(kernel, out_shape=shapes, in_specs=more.pop('in_specs', [V...  17.9 us
    all_gather x1, blocking collectives, shards(): chip = call(core_sum_kernel, left_shape, lax.all_gather(partial, 'core'))  16.2 us

profile of v3, /device:TPU:1, one launch (start us, length us, event | category | flops | bytes accessed | tf_op | source)
XLA Modules:
  0.0 209.7 jit_solution(10084090813489018831)
XLA Ops:
  0.6 3.5 %shard_map.50 = f32[512,128]{1,0:T(8,128)} custom-call(bf16[1,512,896]{2,1,0:T(8,128)(2,1)} %grad.9, bf16[1,512,896]{2,1,0:T(8,128)(2,1)} %error.9, f32[896,128]{1,0:T(8,128)} %q_mat.1), custom_call_target="tpu_custom_call" | custom-call | flops 100000000 | bytes 2555904 | tf_op jit(solution)/shard_map/pallas_call | solution.py:205
  4.1 16.2 %all-gather = f32[1024,128]{1,0:T(8,128)S(1)} all-gather(f32[512,128]{1,0:T(8,128)} %shard_map.50), channel_id=2, replica_groups=mesh['dp'=8,'row'=8,'y'=8,'core'=2] {'core'}, dimensions={0}, use_global_device_ids=true | all-gather | bytes 786432 | tf_op jit(solution)/shard_map/all_gather | solution.py:255
  20.3 0.0 copy-start.1
  20.3 0.0 copy-start
  20.4 23.4 %all_to_all.40.pieces = f32[64,8,128]{2,1,0:T(8,128)S(1)} all-to-all(f32[64,8,128]{2,1,0:T(8,128)S(1)} %shard_map.51), channel_id=1, replica_groups=mesh['dp'=8,'row'=8,'y'=8,'core'=2] {'dp','y'}, dimensions={0} | all-to-all | bytes 524288 | tf_op jit(solution)/shard_map/all_to_all | solution.py:223
  43.8 0.1 shard_map.52
  43.9 17.8 %all_to_all.41.p_mat = f32[64,8,128]{2,1,0:T(8,128)S(1)} all-to-all(f32[64,8,128]{2,1,0:T(8,128)S(1)} %shard_map.52), channel_id=1, replica_groups=mesh['dp'=8,'row'=8,'y'=8,'core'=2] {'dp','y'}, dimensions={0} | all-to-all | bytes 524288 | tf_op jit(solution)/shard_map/all_to_all | solution.py:223
  61.7 0.0 copy-done.1
  61.7 0.0 copy-done
  61.7 1.2 shard_map.53
  62.9 23.6 %all_to_all.42.pieces = f32[64,16,128]{2,1,0:T(8,128)S(1)} all-to-all(f32[64,16,128]{2,1,0:T(8,128)S(1)} %shard_map.53), channel_id=1, replica_groups=mesh['dp'=8,'row'=8,'y'=8,'core'=2] {'dp','row'}, dimensions={0} | all-to-all | bytes 1048576 | tf_op jit(solution)/shard_map/all_to_all | solution.py:223
  86.5 0.1 shard_map.54
  86.6 21.4 %all_to_all.43.both = f32[64,16,128]{2,1,0:T(8,128)S(1)} all-to-all(f32[64,16,128]{2,1,0:T(8,128)S(1)} %shard_map.54), channel_id=1, replica_groups=mesh['dp'=8,'row'=8,'y'=8,'core'=2] {'dp','row'}, dimensions={0} | all-to-all | bytes 1048576 | tf_op jit(solution)/shard_map/all_to_all | solution.py:223
  108.0 5.0 %shard_map.55 = f32[640,128]{1,0:T(8,128)S(1)} custom-call(bf16[1,512,896]{2,1,0:T(8,128)(2,1)S(1)} %copy-done, bf16[1,512,896]{2,1,0:T(8,128)(2,1)S(1)} %copy-done.1, f32[64,16,128]{2,1,0:T(8,128)S(1)} %all_to_all.43.both), custom_call_target="tpu_custom_call" | custom-call | flops 100000000 | bytes 2686976 | tf_op jit(solution)/shard_map/pallas_call | solution.py:205
  113.0 4.2 %all-gather.1 = f32[1280,128]{1,0:T(8,128)S(1)} all-gather(f32[640,128]{1,0:T(8,128)S(1)} %shard_map.55), channel_id=3, replica_groups=mesh['dp'=8,'row'=8,'y'=8,'core'=2] {'core'}, dimensions={0}, use_global_device_ids=true | all-gather | bytes 983040 | tf_op jit(solution)/shard_map/all_gather | solution.py:265
  117.2 20.9 %all_to_all.44.pieces = f32[64,8,128]{2,1,0:T(8,128)S(1)} all-to-all(f32[64,8,128]{2,1,0:T(8,128)S(1)} %get-tuple-element.4), channel_id=1, replica_groups=mesh['dp'=8,'row'=8,'y'=8,'core'=2] {'dp','y'}, dimensions={0} | all-to-all | bytes 524288 | tf_op jit(solution)/shard_map/all_to_all | solution.py:223
  138.2 0.3 shard_map.57
  138.4 17.4 %all_to_all.45.p_mat = f32[64,8,128]{2,1,0:T(8,128)S(1)} all-to-all(f32[64,8,128]{2,1,0:T(8,128)S(1)} %shard_map.57), channel_id=1, replica_groups=mesh['dp'=8,'row'=8,'y'=8,'core'=2] {'dp','y'}, dimensions={0} | all-to-all | bytes 524288 | tf_op jit(solution)/shard_map/all_to_all | solution.py:223
  155.8 1.2 shard_map.58
  157.1 20.8 %all_to_all.46.pieces = f32[64,16,128]{2,1,0:T(8,128)S(1)} all-to-all(f32[64,16,128]{2,1,0:T(8,128)S(1)} %shard_map.58), channel_id=1, replica_groups=mesh['dp'=8,'row'=8,'y'=8,'core'=2] {'dp','row'}, dimensions={0} | all-to-all | bytes 1048576 | tf_op jit(solution)/shard_map/all_to_all | solution.py:223
  177.9 0.1 shard_map.59
  178.0 21.4 %all_to_all.47.both = f32[64,16,128]{2,1,0:T(8,128)S(1)} all-to-all(f32[64,16,128]{2,1,0:T(8,128)S(1)} %shard_map.59), channel_id=1, replica_groups=mesh['dp'=8,'row'=8,'y'=8,'core'=2] {'dp','row'}, dimensions={0} | all-to-all | bytes 1048576 | tf_op jit(solution)/shard_map/all_to_all | solution.py:223
  199.4 3.8 %shard_map.60 = f32[128,128]{1,0:T(8,128)S(1)} custom-call(f32[64,16,128]{2,1,0:T(8,128)S(1)} %all_to_all.47.both), custom_call_target="tpu_custom_call" | custom-call | flops 100000000 | bytes 589824 | tf_op jit(solution)/shard_map/pallas_call | solution.py:205
  203.2 3.8 %all-gather.2 = f32[256,128]{1,0:T(8,128)S(1)} all-gather(f32[128,128]{1,0:T(8,128)S(1)} %shard_map.60), channel_id=4, replica_groups=mesh['dp'=8,'row'=8,'y'=8,'core'=2] {'core'}, dimensions={0}, use_global_device_ids=true | all-gather | bytes 196608 | tf_op jit(solution)/shard_map/all_gather | solution.py:271
  207.0 2.6 %shard_map.61 = (bf16[1,512,896]{2,1,0:T(8,128)(2,1)}, f32[896,128]{1,0:T(8,128)}) custom-call(bf16[1,512,896]{2,1,0:T(8,128)(2,1)S(1)} %copy-done, bf16[1,512,896]{2,1,0:T(8,128)(2,1)S(1)} %copy-done.1, f32[64,8,128]{2,1,0:T(8,128)S(1)} %all_to_all.45.p_mat, f32[64,16,128]{2,1,0:T(8,128)S(1)} %all_to_all.47.both, f32[2,128,128]{2,1,0:T(8,128)S(1)} %bitcast.5), custom_call_target="tpu_custom_call" | custom-call | flops 100000000 | bytes 4128768 | tf_op jit(solution)/shard_map/pallas_call | solution.py:205
  (2 shorter events, 0.1 us)
Async XLA Ops:
  20.3 41.3 %copy-start.1 = (bf16[1,512,896]{2,1,0:T(8,128)(2,1)S(1)}, bf16[1,512,896]{2,1,0:T(8,128)(2,1)}, u32[]{:S(2)}) copy-start(bf16[1,512,896]{2,1,0:T(8,128)(2,1)} %error.9) | copy-start | bytes 2752516
  20.3 41.3 %copy-start = (bf16[1,512,896]{2,1,0:T(8,128)(2,1)S(1)}, bf16[1,512,896]{2,1,0:T(8,128)(2,1)}, u32[]{:S(2)}) copy-start(bf16[1,512,896]{2,1,0:T(8,128)(2,1)} %grad.9) | copy-start | bytes 2752516

commit v4 on v2

--- a/solution.py
+++ b/solution.py
@@ -154,6 +154,12 @@
     out[...] = lower_inverse(gram * by_row * by_lane)
 
 
+def core_half_kernel(partials, out):
+    rows = out.shape[0]
+    start = pl.multiple_of(lax.axis_index("core") * rows, rows)
+    out[...] = partials[0, pl.ds(start, rows), :] + partials[1, pl.ds(start, rows), :]
+
+
 def core_sum_kernel(partials, out):
     out[...] = (partials[0] + partials[1]).reshape(out.shape)
 
@@ -213,10 +219,6 @@
     left_shape = f32(n_left, rows // n_left, rank)
     right_shape = f32(n_right, (cols + rank) // n_right, rank)
 
-    def left_pieces(partial):
-        chip = call(core_sum_kernel, left_shape, lax.all_gather(partial, "core"))
-        return exchange(chip, left_axes)
-
     def right_total(p_all):
         partial = call(functools.partial(right_kernel, scale), right_shape, grad, error, p_all)
         pieces = exchange(partial, right_axes)
@@ -237,12 +239,17 @@
             pltpu.SemaphoreType.DMA,
         ],
     )
-    pieces = left_pieces(partial)
-    p_all = exchange(call(sum_kernel, left_shape, pieces), left_axes)
+    half = rows // lax.axis_size("core")
+    half_shape = f32(n_left, half // n_left, rank)
+    mine = call(core_half_kernel, f32(half, rank), lax.all_gather(partial, "core"))
+    pieces = exchange(mine.reshape(half_shape.shape), left_axes)
+    mine = exchange(call(sum_kernel, half_shape, pieces), left_axes).reshape(half, rank)
+    p_all = lax.all_gather(mine, "core", tiled=True).reshape(left_shape.shape)
     both = right_total(p_all)
     partial = call(functools.partial(next_left_kernel, scale), f32(rows, rank), grad, error, both)
     inverse = call(inverse_kernel, f32(rank, rank), both, flops=4 * 10**9)
-    pieces = left_pieces(partial)
+    chip = call(core_sum_kernel, left_shape, lax.all_gather(partial, "core"))
+    pieces = exchange(chip, left_axes)
     p_all = exchange(call(sum_scale_kernel, left_shape, pieces, inverse), left_axes)
     both = right_total(p_all)
     return call(

time: 209 us -> 210 us (level)
  the two profiles are of different devices: /device:TPU:16 before, /device:TPU:2 now
where the time goes in v4:
time: 210 us
  blocking collectives  174 us (83%)
  Pallas kernels  19.4 us (9%)
  waiting for transfers between devices  11 us (5%)
  starting transfers between devices  4.62 us (2%)
    all_to_all x7, blocking collectives, exchange(): return lax.all_to_all(x, axes, 0, 0, tiled=True)  168 us
    pallas_call x12, Pallas kernels, call(): pl.pallas_call(kernel, out_shape=shapes, in_specs=more.pop('in_specs', [V...  19.4 us
    all_to_all x1, waiting for transfers between devices, exchange(): return lax.all_to_all(x, axes, 0, 0, tiled=True)  11 us
    all_to_all x1, starting transfers between devices, exchange(): return lax.all_to_all(x, axes, 0, 0, tiled=True)  4.62 us
  transfers between devices with their start and end apart: 1, of which 1 were waited for; matrix products, arithmetic and copies ran while one was open for 0% of the time, Pallas kernels for 2%

profile of v4, /device:TPU:2, one launch (start us, length us, event | category | flops | bytes accessed | tf_op | source)
XLA Modules:
  0.0 209.9 jit_solution(9737919244352932137)
XLA Ops:
  0.6 3.5 %shard_map.50 = f32[512,128]{1,0:T(8,128)} custom-call(bf16[1,512,896]{2,1,0:T(8,128)(2,1)} %grad.9, bf16[1,512,896]{2,1,0:T(8,128)(2,1)} %error.9, f32[896,128]{1,0:T(8,128)} %q_mat.1), custom_call_target="tpu_custom_call" | custom-call | flops 100000000 | bytes 2555904 | tf_op jit(solution)/shard_map/pallas_call | solution.py:192
  4.1 2.4 %all-gather = f32[1024,128]{1,0:T(8,128)S(1)} all-gather(f32[512,128]{1,0:T(8,128)} %shard_map.50), channel_id=2, replica_groups=mesh['dp'=8,'row'=8,'y'=8,'core'=2] {'core'}, dimensions={0}, use_global_device_ids=true | all-gather | bytes 786432 | tf_op jit(solution)/shard_map/all_gather | solution.py:244
  6.5 0.0 copy-start
  6.5 0.0 copy-start.1
  6.6 36.2 %all_to_all.40.pieces = f32[64,4,128]{2,1,0:T(4,128)S(1)} all-to-all(f32[64,4,128]{2,1,0:T(4,128)S(1)} %bitcast.8), channel_id=1, replica_groups=mesh['dp'=8,'row'=8,'y'=8,'core'=2] {'dp','y'}, dimensions={0} | all-to-all | bytes 262144 | tf_op jit(solution)/shard_map/all_to_all | solution.py:210
  42.8 0.1 shard_map.52
  42.9 16.6 %all_to_all.41 = f32[64,4,128]{2,1,0:T(4,128)S(1)} all-to-all(f32[64,4,128]{2,1,0:T(4,128)S(1)} %shard_map.52), channel_id=1, replica_groups=mesh['dp'=8,'row'=8,'y'=8,'core'=2] {'dp','y'}, dimensions={0} | all-to-all | bytes 262144 | tf_op jit(solution)/shard_map/all_to_all | solution.py:210
  59.4 2.0 all_gather.17
  61.4 0.0 copy-done
  61.4 0.0 copy-done.1
  61.4 1.2 shard_map.53
  62.6 27.6 %all_to_all.42.pieces = f32[64,16,128]{2,1,0:T(8,128)S(1)} all-to-all(f32[64,16,128]{2,1,0:T(8,128)S(1)} %shard_map.53), channel_id=1, replica_groups=mesh['dp'=8,'row'=8,'y'=8,'core'=2] {'dp','row'}, dimensions={0} | all-to-all | bytes 1048576 | tf_op jit(solution)/shard_map/all_to_all | solution.py:210
  90.2 0.1 shard_map.54
  90.3 24.3 %all_to_all.43.both = f32[64,16,128]{2,1,0:T(8,128)S(1)} all-to-all(f32[64,16,128]{2,1,0:T(8,128)S(1)} %shard_map.54), channel_id=1, replica_groups=mesh['dp'=8,'row'=8,'y'=8,'core'=2] {'dp','row'}, dimensions={0} | all-to-all | bytes 1048576 | tf_op jit(solution)/shard_map/all_to_all | solution.py:210
  114.7 1.2 shard_map.55
  115.9 2.2 %all-gather.1 = f32[1024,128]{1,0:T(8,128)S(1)} all-gather(f32[512,128]{1,0:T(8,128)S(1)} %shard_map.55), channel_id=3, replica_groups=mesh['dp'=8,'row'=8,'y'=8,'core'=2] {'core'}, dimensions={0}, use_global_device_ids=true | all-gather | bytes 786432 | tf_op jit(solution)/shard_map/all_gather | solution.py:251
  118.1 0.7 shard_map.56
  118.8 4.6 %all-to-all-start.4 = ((f32[64,8,128]{2,1,0:T(8,128)}), f32[64,8,128]{2,1,0:T(8,128)S(1)}, u32[]{:S(2)}, u32[]{:S(2)}) async-start(f32[64,8,128]{2,1,0:T(8,128)} %shard_map.56), calls=%async_computation.4 | async-start | bytes 524288 | tf_op jit(solution)/shard_map/all_to_all | solution.py:210
  123.4 4.5 %shard_map.57.inverse = f32[128,128]{1,0:T(8,128)S(1)} custom-call(f32[64,16,128]{2,1,0:T(8,128)S(1)} %all_to_all.43.both), custom_call_target="tpu_custom_call" | custom-call | flops 4000000000 | bytes 589824 | tf_op jit(solution)/shard_map/pallas_call | solution.py:192
  128.0 11.0 %all-to-all-done.4.pieces = f32[64,8,128]{2,1,0:T(8,128)S(1)} async-done(((f32[64,8,128]{2,1,0:T(8,128)}), f32[64,8,128]{2,1,0:T(8,128)S(1)}, u32[]{:S(2)}, u32[]{:S(2)}) %all-to-all-start.4) | async-done | bytes 262176 | tf_op jit(solution)/shard_map/all_to_all | solution.py:210
  138.9 0.3 shard_map.58
  139.2 18.5 %all_to_all.44.p_mat = f32[64,8,128]{2,1,0:T(8,128)S(1)} all-to-all(f32[64,8,128]{2,1,0:T(8,128)S(1)} %shard_map.58), channel_id=1, replica_groups=mesh['dp'=8,'row'=8,'y'=8,'core'=2] {'dp','y'}, dimensions={0} | all-to-all | bytes 524288 | tf_op jit(solution)/shard_map/all_to_all | solution.py:210
  157.7 1.2 shard_map.59
  158.9 22.8 %all_to_all.45.pieces = f32[64,16,128]{2,1,0:T(8,128)S(1)} all-to-all(f32[64,16,128]{2,1,0:T(8,128)S(1)} %shard_map.59), channel_id=1, replica_groups=mesh['dp'=8,'row'=8,'y'=8,'core'=2] {'dp','row'}, dimensions={0} | all-to-all | bytes 1048576 | tf_op jit(solution)/shard_map/all_to_all | solution.py:210
  181.8 0.1 shard_map.60
  181.9 21.5 %all_to_all.46.both = f32[64,16,128]{2,1,0:T(8,128)S(1)} all-to-all(f32[64,16,128]{2,1,0:T(8,128)S(1)} %shard_map.60), channel_id=1, replica_groups=mesh['dp'=8,'row'=8,'y'=8,'core'=2] {'dp','row'}, dimensions={0} | all-to-all | bytes 1048576 | tf_op jit(solution)/shard_map/all_to_all | solution.py:210
  203.4 6.4 %shard_map.61 = (bf16[1,512,896]{2,1,0:T(8,128)(2,1)}, f32[896,128]{1,0:T(8,128)}) custom-call(bf16[1,512,896]{2,1,0:T(8,128)(2,1)S(1)} %copy-done, bf16[1,512,896]{2,1,0:T(8,128)(2,1)S(1)} %copy-done.1, f32[64,8,128]{2,1,0:T(8,128)S(1)} %all_to_all.44.p_mat, f32[64,16,128]{2,1,0:T(8,128)S(1)} %all_to_all.46.both), custom_call_target="tpu_custom_call" | custom-call | flops 100000000 | bytes 3997696 | tf_op jit(solution)/shard_map/pallas_call | solution.py:192
  (1 shorter events, 0.0 us)
Async XLA Ops:
  6.5 54.9 %copy-start = (bf16[1,512,896]{2,1,0:T(8,128)(2,1)S(1)}, bf16[1,512,896]{2,1,0:T(8,128)(2,1)}, u32[]{:S(2)}) copy-start(bf16[1,512,896]{2,1,0:T(8,128)(2,1)} %grad.9) | copy-start | bytes 2752516
  6.5 54.9 %copy-start.1 = (bf16[1,512,896]{2,1,0:T(8,128)(2,1)S(1)}, bf16[1,512,896]{2,1,0:T(8,128)(2,1)}, u32[]{:S(2)}) copy-start(bf16[1,512,896]{2,1,0:T(8,128)(2,1)} %error.9) | copy-start | bytes 2752516
  118.8 20.1 %all-to-all-start.4 = ((f32[64,8,128]{2,1,0:T(8,128)}), f32[64,8,128]{2,1,0:T(8,128)S(1)}, u32[]{:S(2)}, u32[]{:S(2)}) async-start(f32[64,8,128]{2,1,0:T(8,128)} %shard_map.56), calls=%async_computation.4 | async-start | bytes 524288 | tf_op jit(solution)/shard_map/all_to_all | solution.py:210
